TPU v7x, 32 devices: a whole 2x2x4 slice. The times are simulated.
32 devices in a mesh: freq: 8 (over y, x, core), slab: 4 (over z).
Axes of the slice: x: 2, y: 2, z: 4, core: 2. Of those that a mesh axis runs over, the one named last changes fastest.
Arguments:
- traces: bfloat16 [98304, 2048], P(('freq', 'slab')), may hold values from -6 to 6
- trace_counts: int32 [32, 8], P(('freq', 'slab')), may hold values from 1 to 512, 3072 in all within a row
- aperture_start: int32 [256], P(('freq', 'slab')), may hold values from 0 to 511
- shot_position: int32 [256], P(('freq', 'slab')), may hold values from 0 to 4095
- rec_slot: int32 [512], replicated, may hold values from 0 to 767, as said below
Outputs:
- encoded: bfloat16 [768, 256, 256], P('slab', 'freq')
Inputs may be any that keep to these rules, and one draw needn't show every extreme that they name: `rec_slot`: distinct receivers have distinct slots. No depth slab owns more than 192 receivers, at least one owns exactly 192, and slots 0 and 767 are always used.
All inputs are finite; a program needn't handle non-finite values.
Results may differ from a plain program's by a relative error of at most 0.0062.
Values may be sent and summed in bfloat16 or wider, within the bound.
A program may use at most 192 MiB of HBM per device.

v0:
```python
import math

import jax
import jax.numpy as jnp
from jax import lax
from jax.sharding import PartitionSpec as P

NT = 2048
FREQUENCY_COUNT = 256
F0 = 8
RAY_PARAM_COUNT = 128
NREC = 512
RDIV = 16


def dft_factors(freq_bins, samples):
    sample_index = jnp.arange(samples, dtype=jnp.int32)
    phase_index = jnp.remainder(sample_index[:, None] * freq_bins[None, :], samples)
    angle_rad = phase_index.astype(jnp.float32) * (2.0 * math.pi / samples)
    factor = 1.0 / math.sqrt(samples)
    return (
        (jnp.cos(angle_rad) * factor).astype(jnp.bfloat16),
        (-jnp.sin(angle_rad) * factor).astype(jnp.bfloat16),
    )


def phase_blocks(freq_bins, positions, total_shots):
    ray_offset = jnp.arange(RAY_PARAM_COUNT, dtype=jnp.int32) - RAY_PARAM_COUNT // 2
    period = NT * RDIV
    product = (
        freq_bins[:, None, None, None]
        * ray_offset[None, None, None, :]
        * positions[None, :, :, None]
    )
    angle_rad = jnp.remainder(product, period).astype(jnp.float32) * (2.0 * math.pi / period)
    factor = 1.0 / math.sqrt(total_shots)
    cosine = (jnp.cos(angle_rad) * factor).astype(jnp.bfloat16)
    sine_part = (jnp.sin(angle_rad) * factor).astype(jnp.bfloat16)
    upper_half = jnp.concatenate([cosine, -sine_part], axis=3)
    lower_half = jnp.concatenate([sine_part, cosine], axis=3)
    stacked = jnp.stack([upper_half, lower_half], axis=2)
    return stacked.reshape(
        freq_bins.shape[0], positions.shape[0] * 2 * positions.shape[1], 2 * RAY_PARAM_COUNT
    )


def frequency_spectra(transform, traces):
    return lax.dot_general(
        transform, traces, (((0,), (1,)), ((), ())), preferred_element_type=jnp.float32
    ).astype(jnp.bfloat16)


def receiver_index(counts, starts, row_total, shot_total):
    shot_count = counts.shape[0]
    by_source = counts.reshape(shot_count // shot_total, shot_total)
    inclusive = jnp.cumsum(by_source, axis=1)
    source_base = (jnp.arange(shot_count // shot_total, dtype=jnp.int32) * row_total)[:, None]
    begins = (source_base + inclusive - by_source).reshape(shot_count)
    receivers = jnp.arange(NREC, dtype=jnp.int32)
    offset = jnp.remainder(receivers[None, :] - starts[:, None], NREC)
    valid = offset < counts[:, None]
    picks = jnp.where(valid, begins[:, None] + offset, 0)
    return (picks, valid)


def slot_matrix(rec_slot, slot_count):
    return (rec_slot[:, None] == jnp.arange(slot_count, dtype=jnp.int32)[None, :]).astype(
        jnp.bfloat16
    )


def slot_grid(
    owned_spectra, counts, starts, row_total, shot_total, slot_count, freq_block, rec_slot
):
    picks, valid = receiver_index(counts, starts, row_total, shot_total)
    shot_count = counts.shape[0]
    picked = jnp.take(owned_spectra, picks.reshape(-1), axis=1)
    picked = picked.reshape(2, freq_block, shot_count, NREC)
    picked = jnp.where(valid[None, None, :, :], picked, jnp.zeros((), jnp.bfloat16))
    lattice = jnp.einsum(
        "rs,cfhr->sfch",
        slot_matrix(rec_slot, slot_count),
        picked,
        preferred_element_type=jnp.float32,
    )
    return lattice.astype(jnp.bfloat16).reshape(slot_count, freq_block, 2 * shot_count)


def on_device(traces, trace_counts, aperture_start, shot_position, rec_slot):
    row_total, samples = traces.shape
    shot_total = trace_counts.shape[1]
    freq_groups = lax.axis_size("freq")
    slab_groups = lax.axis_size("slab")
    freq_block = FREQUENCY_COUNT // freq_groups
    slot_cap = 3 * NREC // (2 * slab_groups)
    slot_count = slot_cap * slab_groups
    all_shots = shot_total * freq_groups * slab_groups
    column = jnp.arange(2 * FREQUENCY_COUNT, dtype=jnp.int32)
    owner_block = column // (2 * freq_block)
    within = column % (2 * freq_block)
    column_bins = F0 + owner_block * freq_block + within % freq_block
    cosine_table, sine_table = dft_factors(column_bins, samples)
    transform = jnp.where((within // freq_block == 0)[None, :], cosine_table, sine_table)
    local_bins = F0 + lax.axis_index("freq") * freq_block + jnp.arange(freq_block, dtype=jnp.int32)
    own_counts = trace_counts[0]
    spectra = frequency_spectra(transform, traces)
    holder_counts, holder_starts, holder_positions = (
        lax.all_gather(own_counts, "freq", axis=0, tiled=True),
        lax.all_gather(aperture_start, "freq", axis=0, tiled=True),
        lax.all_gather(shot_position, "freq", axis=0, tiled=True),
    )
    owned_spectra = lax.all_to_all(spectra, "freq", split_axis=0, concat_axis=1, tiled=True)
    filled_lattice = slot_grid(
        owned_spectra,
        holder_counts,
        holder_starts,
        row_total,
        shot_total,
        slot_count,
        freq_block,
        rec_slot,
    )
    phases = phase_blocks(local_bins, holder_positions[None, :], all_shots)
    summed = lax.psum_scatter(
        jnp.einsum("xfs,fsq->xfq", filled_lattice, phases, preferred_element_type=jnp.float32),
        "slab",
        scatter_dimension=0,
        tiled=True,
    )
    return summed.astype(jnp.bfloat16)


def solution(mesh):
    return jax.shard_map(
        on_device,
        mesh=mesh,
        in_specs=(
            P(("freq", "slab"), None),
            P(("freq", "slab"), None),
            P(("freq", "slab")),
            P(("freq", "slab")),
            P(),
        ),
        out_specs=P("slab", "freq", None),
        check_vma=False,
    )
```

profile of v0, /device:TPU:1, one launch (start us, length us, event | category | flops | bytes accessed | tf_op | source)
XLA Modules:
  0.0 695.0 jit_solution(16395539354288926045)
XLA Ops:
  6.6 28.7 %convolution_convert_fusion = bf16[512,3072]{1,0:T(8,128)(2,1)} fusion(bf16[3072,2048]{1,0:T(8,128)(2,1)} %param.5, s32[512]{0:T(512)S(1)} %fusion.42, pred[512]{0:T(512)(128)(4,1)S(1)} %fusion.38), kind=kOutput, calls=%fused_computation.6 | convolution fusion | flops 6464995328 | bytes 15731200 | tf_op jit(solution)/shard_map/dot_general | solution.py:48
  35.3 5.5 all-to-all-start
  40.8 0.6 dynamic-slice
  42.1 0.2 dynamic-update-slice
  42.4 0.2 dynamic-update-slice.1
  42.6 36.6 %all-reduce.3 = (s32[64]{0:T(128)S(1)}, s32[64]{0:T(128)S(1)}, s32[64]{0:T(128)S(1)}) all-reduce(s32[64]{0:T(128)S(1)} %dynamic-update-slice, s32[64]{0:T(128)S(1)} %bitcast_dynamic-update-slice_fusion, s32[64]{0:T(128)S(1)} %dynamic-update-slice.1), channel_id=1, replica_groups=mesh['freq'=8,'slab'=4] {'freq'}, use_global_device_ids=true, to_apply=%add | all-reduce | flops 192 | bytes 1536
  79.3 0.2 reduce_window_sum.11
  79.7 0.1 copy.29
  80.2 0.6 compare_select_fusion
  80.9 4.2 fusion.37
  85.1 4.6 multiply_convert_fusion.3
  89.7 0.3 maximum_bitcast_fusion
  90.0 0.2 pad_maximum_fusion
  90.4 0.2 broadcast_compare_fusion
  90.6 6.6 copy.18
  97.2 113.8 %gather_fusion = bf16[32768,64]{1,0:T(8,128)(2,1)} fusion(bf16[64,24576]{0,1:T(8,128)(2,1)} %bitcast.53, s32[32768]{0:T(1024)S(1)} %broadcast_clamp_fusion), kind=kCustom, calls=%fused_computation | custom fusion | bytes 8519680 | tf_op jit(solution)/shard_map/jit(_take)/gather | solution.py:77
  211.0 8.6 %copy.19 = bf16[64,32768]{1,0:T(8,128)(2,1)} copy(bf16[64,32768]{0,1:T(8,128)(2,1)} %bitcast.55) | data formatting | bytes 8388608 | tf_op jit(solution)/shard_map/jit(_take)/gather | solution.py:77
  219.6 3.8 copy.30
  223.4 5.8 convert_bitcast_fusion
  229.2 3.2 copy.20
  232.4 10.1 %convolution_bitcast_fusion = f32[768,32,256]{0,2,1:T(8,128)} fusion(bf16[32,128,256]{2,1,0:T(8,128)(2,1)S(1)} %bitcast.57, bf16[768,32,128]{0,2,1:T(8,128)(2,1)S(1)} %bitcast.54), kind=kOutput, calls=%fused_computation.1 | convolution fusion | flops 1610612736 | bytes 33554432 | tf_op jit(solution)/shard_map/xfs,fsq->xfq/dot_general | solution.py:125
  242.5 25.1 %copy.23 = f32[768,32,256]{2,1,0:T(8,128)} copy(f32[768,32,256]{0,2,1:T(8,128)} %convolution_bitcast_fusion) | data formatting | bytes 50331648 | tf_op jit(solution)/shard_map/xfs,fsq->xfq/transpose | solution.py:125
  267.6 415.6 %reduce-scatter.2.cloned.1.call-done = f32[192,32,256]{2,1,0:T(8,128)} async-done(((f32[768,32,256]{2,1,0:T(8,128)}), f32[192,32,256]{2,1,0:T(8,128)}) %reduce-scatter.2.cloned.1.call-update) | async-done | bytes 6291472 | tf_op jit(solution)/shard_map/reduce_scatter | solution.py:124
  683.2 4.9 convert_element_type.76
  (33 shorter events, 1.1 us)
Async XLA Ops:
  35.3 5.6 copy-start.4
  35.3 6.7 copy-start.1
  35.3 6.9 copy-start.2
  35.3 7.1 %copy-start.3 = (s32[8]{0:T(128)S(1)}, s32[8]{0:T(128)}, u32[]{:S(2)}) copy-start(s32[8]{0:T(128)} %param.7) | copy-start | bytes 100
  35.3 55.3 %all-to-all-start = ((bf16[8,64,3072]{2,1,0:T(8,128)(2,1)}), bf16[8,64,3072]{2,1,0:T(8,128)(2,1)}, u32[]{:S(2)}, u32[]{:S(2)}) async-start(bf16[8,64,3072]{2,1,0:T(8,128)(2,1)} %bitcast.5), calls=%async_computation | async-start | bytes 6291456 | tf_op jit(solution)/shard_map/all_to_all | solution.py:112
  40.8 642.4 %reduce-scatter.2.cloned.1.call-start = ((), (), s32[]{:S(2)}) async-start(), calls=%async_computation.2 | async-start | bytes 31457280 | tf_op jit(solution)/shard_map/reduce_scatter | solution.py:124
  219.6 3.8 copy-start
Sparse Core Ops, SparseCore 0:
  267.7 415.4 reduce-scatter.1
where the time goes:
time: 697 us; the launch traced here: 695 us
  waiting for transfers between devices  416 us (60%)
  local copies, waits for them, and re-layouts  163 us (23%)
  matrix products  44.6 us (6%)
  blocking collectives  36.6 us (5%)
  other arithmetic  15.5 us (2%)
  between operations  14.2 us (2%)
    reduce_scatter x1, waiting for transfers between devices, on_device(): lax.psum_scatter(jnp.einsum('xfs,fsq->xfq', filled_lattice, phases, prefe...  416 us
    gather x2, local copies, waits for them, and re-layouts, slot_grid(): picked = jnp.take(owned_spectra, picks.reshape(-1), axis=1)  122 us
    unnamed x1, blocking collectives  36.6 us
    dot_general x1, matrix products, frequency_spectra(): lax.dot_general(transform, traces, (((0,), (1,)), ((), ())), preferred_el...  28.7 us
    transpose x1, local copies, waits for them, and re-layouts, on_device(): jnp.einsum('xfs,fsq->xfq', filled_lattice, phases, preferred_element_type...  25.1 us
  transfers between devices with their start and end apart: 2, of which 1 were waited for; matrix products, arithmetic and copies ran while one was open for 2% of the time, Pallas kernels for 0%

commit v1 on v0

v1 whole, which is shorter than its diff:
```python
import functools
import math

import jax
import jax.numpy as jnp
import ml_dtypes
import numpy as np
from jax import lax
from jax.experimental import pallas as pl
from jax.experimental.pallas import tpu as pltpu
from jax.sharding import PartitionSpec as P

NT = 2048
FREQUENCY_COUNT = 256
F0 = 8
RAY_PARAM_COUNT = 128
NREC = 512
RDIV = 16
LANES = 128
HALF = 64
VMEM_BYTES = 56 * 1024 * 1024


def dft_table(samples):
    bins = F0 + np.arange(FREQUENCY_COUNT, dtype=np.int64)
    index = (bins[:, None] * np.arange(samples, dtype=np.int64)[None, :]) % samples
    angle = index.astype(np.float64) * (2.0 * math.pi / samples)
    factor = 1.0 / math.sqrt(samples)
    table = np.concatenate([np.cos(angle), -np.sin(angle)], axis=0) * factor
    return table.astype(np.float32).astype(ml_dtypes.bfloat16)


def column_slots(slabs, cap):
    whole, rest = cap // LANES, cap % LANES
    assert rest <= HALF
    parts = []
    for slab in range(slabs):
        parts.append(slab * cap + np.arange(whole * LANES))
    for slab in range(slabs if rest else 0):
        lane = np.arange(HALF)
        parts.append(np.where(lane < rest, slab * cap + whole * LANES + lane, -2))
    return np.concatenate(parts).astype(np.int32)


def lattice_kernel(
    slabs, whole, rest, freq_groups, shots, row_steps, window,
    starts, counts, begins, inverse, table, traces, out, spectra, full, part,
):
    step = pl.program_id(0)
    rows = traces.shape[0]
    freq_block = FREQUENCY_COUNT // freq_groups
    pair = freq_block // 2
    block = lax.dot_general(
        table[...], traces[...], (((1,), (1,)), ((), ())), preferred_element_type=jnp.float32
    ).astype(jnp.bfloat16)
    spectra[:, pl.ds(pl.multiple_of(step * rows, rows), rows)] = block

    @pl.when(step == row_steps - 1)
    def _place():
        total = row_steps * rows
        columns = inverse.shape[1]
        full_columns = slabs * whole * LANES
        lane = lax.broadcasted_iota(jnp.int32, (FREQUENCY_COUNT // 2, LANES), 1)

        def one_shot(k, carry):
            begin = begins[k]
            base = pl.multiple_of(
                jnp.minimum((begin // LANES) * LANES, total - window), LANES
            )
            piece = spectra[:, pl.ds(base, window)]
            for first in range(0, columns, 2 * LANES):
                inv = inverse[:, first : first + 2 * LANES]
                offset = jnp.bitwise_and(inv - starts[k], NREC - 1)
                valid = (inv >= 0) & (offset < counts[k])
                target = jnp.where(valid, offset + (begin - base), -1)
                line = lax.broadcasted_iota(jnp.int32, (window, 2 * LANES), 0)
                hot = jnp.where(line == target, 1.0, 0.0).astype(jnp.bfloat16)
                placed = jnp.dot(piece, hot, preferred_element_type=jnp.float32)
                for half in range(2):
                    at = first + half * LANES
                    value = placed[:, half * LANES : (half + 1) * LANES]
                    for c in range(2):
                        mine = value[c * FREQUENCY_COUNT : (c + 1) * FREQUENCY_COUNT]
                        if at < full_columns:
                            full[
                                at // LANES,
                                pl.ds(c * shots + k, FREQUENCY_COUNT, stride=2 * shots),
                                :,
                            ] = mine
                            continue
                        slab = (at - full_columns) // HALF
                        split = mine.reshape(freq_groups, 2, pair, LANES)
                        low = split[:, 0].reshape(freq_groups * pair, LANES)
                        high = split[:, 1].reshape(freq_groups * pair, LANES)
                        spot = pl.ds(c * shots + k, freq_groups * pair, stride=2 * shots)
                        part[slab, spot, :] = jnp.where(lane < HALF, low, pltpu.roll(high, HALF, 1))
                        part[slab + 1, spot, :] = jnp.where(
                            lane < HALF, pltpu.roll(low, HALF, 1), high
                        )
            return carry

        lax.fori_loop(0, shots, one_shot, 0)
        full_rows = freq_block * 2 * shots
        part_rows = pair * 2 * shots

        def deliver(group, carry):
            for slab in range(slabs):
                dest = group * slabs + slab
                for w in range(whole):
                    out[dest, w * full_rows : (w + 1) * full_rows, :] = full[
                        slab * whole + w,
                        pl.ds(pl.multiple_of(group * full_rows, full_rows), full_rows),
                        :,
                    ].astype(jnp.bfloat16)
                if rest:
                    out[dest, whole * full_rows : whole * full_rows + part_rows, :] = part[
                        slab,
                        pl.ds(pl.multiple_of(group * part_rows, part_rows), part_rows),
                        :,
                    ].astype(jnp.bfloat16)
            return carry

        lax.fori_loop(0, freq_groups, deliver, 0)


def make_lattice(traces, counts, starts, rec_slot, slabs, cap, freq_groups):
    row_total, samples = traces.shape
    shots = counts.shape[0]
    whole, rest = cap // LANES, cap % LANES
    rows = 256
    row_steps = row_total // rows
    window = NREC + LANES
    freq_block = FREQUENCY_COUNT // freq_groups
    dest_rows = (whole * freq_block + (freq_block // 2 if rest else 0)) * 2 * shots
    slots = jnp.asarray(column_slots(slabs, cap))
    receivers = jnp.arange(NREC, dtype=jnp.int32)
    inverse = jnp.max(
        jnp.where(rec_slot[:, None] == slots[None, :], receivers[:, None], -1), axis=0
    )[None, :]
    begins = jnp.cumsum(counts) - counts
    smem = pl.BlockSpec(memory_space=pltpu.SMEM)
    return pl.pallas_call(
        functools.partial(
            lattice_kernel, slabs, whole, rest, freq_groups, shots, row_steps, window
        ),
        grid=(row_steps,),
        in_specs=[
            smem,
            smem,
            smem,
            pl.BlockSpec(inverse.shape, lambda i: (0, 0)),
            pl.BlockSpec((2 * FREQUENCY_COUNT, samples), lambda i: (0, 0)),
            pl.BlockSpec((rows, samples), lambda i: (i, 0)),
        ],
        out_specs=pl.BlockSpec((freq_groups * slabs, dest_rows, LANES), lambda i: (0, 0, 0)),
        out_shape=jax.ShapeDtypeStruct(
            (freq_groups * slabs, dest_rows, LANES), jnp.bfloat16
        ),
        scratch_shapes=[
            pltpu.VMEM((2 * FREQUENCY_COUNT, row_total), jnp.bfloat16),
            pltpu.VMEM((max(slabs * whole, 1), FREQUENCY_COUNT * 2 * shots, LANES), jnp.float32),
            pltpu.VMEM((slabs, FREQUENCY_COUNT * shots, LANES), jnp.float32),
        ],
        compiler_params=pltpu.CompilerParams(vmem_limit_bytes=VMEM_BYTES),
        cost_estimate=pl.CostEstimate(
            flops=2 * row_total * samples * 2 * FREQUENCY_COUNT,
            bytes_accessed=row_total * samples * 2,
            transcendentals=0,
        ),
        name="lattice",
    )(starts, counts, begins, inverse, jnp.asarray(dft_table(samples)), traces)


def cos_sin(q, period):
    quarter = period // 4
    shifted = q + quarter // 2
    quadrant = jnp.bitwise_and(shifted // quarter, 3)
    x = (jnp.bitwise_and(shifted, quarter - 1) - quarter // 2).astype(jnp.float32) * (
        2.0 * math.pi / period
    )
    x2 = x * x
    sine = x + x * x2 * (
        -1.6666666666e-1 + x2 * (8.3333333e-3 + x2 * (-1.98412698e-4 + x2 * 2.7557319e-6))
    )
    cosine = 1.0 + x2 * (
        -0.5 + x2 * (4.16666667e-2 + x2 * (-1.38888889e-3 + x2 * 2.48015873e-5))
    )
    swap = jnp.bitwise_and(quadrant, 1) == 1
    c = jnp.where(swap, sine, cosine)
    s = jnp.where(swap, cosine, sine)
    c = jnp.where((quadrant == 1) | (quadrant == 2), -c, c)
    s = jnp.where(quadrant >= 2, -s, s)
    return c, s


def phase_kernel(shots, total_shots, first_bin, positions, out):
    bin_index = first_bin[0] + pl.program_id(0)
    rays = lax.broadcasted_iota(jnp.int32, positions.shape, 1) - RAY_PARAM_COUNT // 2
    period = NT * RDIV
    q = jnp.bitwise_and(bin_index * rays * positions[...], period - 1)
    c, s = cos_sin(q, period)
    factor = 1.0 / math.sqrt(total_shots)
    sources = positions.shape[0] // shots
    c = (c * factor).reshape(sources, 1, shots, RAY_PARAM_COUNT)
    s = (s * factor).reshape(sources, 1, shots, RAY_PARAM_COUNT)
    left = jnp.concatenate([c, s], axis=1).reshape(sources * 2 * shots, RAY_PARAM_COUNT)
    right = jnp.concatenate([-s, c], axis=1).reshape(sources * 2 * shots, RAY_PARAM_COUNT)
    out[0, :, :RAY_PARAM_COUNT] = left.astype(jnp.bfloat16)
    out[0, :, RAY_PARAM_COUNT:] = right.astype(jnp.bfloat16)


def make_phases(positions, first_bin, freq_block, shots):
    total_shots = positions.shape[0]
    wide = jnp.broadcast_to(positions[:, None], (total_shots, RAY_PARAM_COUNT))
    return pl.pallas_call(
        functools.partial(phase_kernel, shots, total_shots),
        grid=(freq_block,),
        in_specs=[
            pl.BlockSpec(memory_space=pltpu.SMEM),
            pl.BlockSpec((total_shots, RAY_PARAM_COUNT), lambda i: (0, 0)),
        ],
        out_specs=pl.BlockSpec((1, 2 * total_shots, 2 * RAY_PARAM_COUNT), lambda i: (i, 0, 0)),
        out_shape=jax.ShapeDtypeStruct(
            (freq_block, 2 * total_shots, 2 * RAY_PARAM_COUNT), jnp.bfloat16
        ),
        compiler_params=pltpu.CompilerParams(vmem_limit_bytes=VMEM_BYTES),
        cost_estimate=pl.CostEstimate(
            flops=freq_block * total_shots * RAY_PARAM_COUNT * 40,
            bytes_accessed=freq_block * total_shots * 8 * RAY_PARAM_COUNT,
            transcendentals=0,
        ),
        name="phases",
    )(first_bin, wide)


def encode_kernel(cap, whole, rest, pair, *refs):
    blocks = refs[: 2 * whole + (1 if rest else 0)]
    low_phase, high_phase, out, summed = refs[len(blocks) :]
    step = pl.program_id(0)
    freq_block = 2 * pair
    depth = low_phase.shape[1]
    over_rows = (((0,), (0,)), ((), ()))

    def put(slot, f, value):
        spot = pl.ds(slot * freq_block + f, value.shape[0], stride=freq_block)
        for half in range(2):
            summed[half, spot, :] = value[:, half * LANES : (half + 1) * LANES]

    for w in range(whole):
        for side, phase in enumerate((low_phase, high_phase)):
            held = blocks[2 * w + side][...].reshape(depth, LANES)
            value = lax.dot_general(
                held, phase[0], over_rows, preferred_element_type=jnp.float32
            )
            put(w * LANES, step + side * pair, value)
    if rest:
        held = blocks[2 * whole][...].reshape(depth, LANES)
        for side, phase in enumerate((low_phase, high_phase)):
            value = lax.dot_general(
                held, phase[0], over_rows, preferred_element_type=jnp.float32
            )
            put(whole * LANES, step + side * pair, value[side * HALF : side * HALF + rest])

    @pl.when(step == pair - 1)
    def _round():
        chunk = 16

        def one(i, carry):
            for half in range(2):
                value = summed[
                    half, pl.ds(pl.multiple_of(i * chunk * freq_block, 8), chunk * freq_block), :
                ]
                out[pl.ds(i * chunk, chunk), :, half * LANES : (half + 1) * LANES] = value.reshape(
                    chunk, freq_block, LANES
                ).astype(jnp.bfloat16)
            return carry

        lax.fori_loop(0, cap // chunk, one, 0)


def encode(received, phases, cap, freq_block, shots):
    sources = received.shape[0]
    whole, rest = cap // LANES, cap % LANES
    pair = freq_block // 2
    group = 2 * shots
    held = received.reshape(sources, -1, group, LANES)

    def spec(first):
        return pl.BlockSpec((sources, 1, group, LANES), lambda i: (0, first + i, 0, 0))

    firsts = []
    for w in range(whole):
        firsts += [w * freq_block, w * freq_block + pair]
    if rest:
        firsts.append(whole * freq_block)
    depth = phases.shape[1]
    return pl.pallas_call(
        functools.partial(encode_kernel, cap, whole, rest, pair),
        grid=(pair,),
        in_specs=[spec(first) for first in firsts]
        + [
            pl.BlockSpec((1, depth, 2 * RAY_PARAM_COUNT), lambda i: (i, 0, 0)),
            pl.BlockSpec((1, depth, 2 * RAY_PARAM_COUNT), lambda i: (i + pair, 0, 0)),
        ],
        out_specs=pl.BlockSpec((cap, freq_block, 2 * RAY_PARAM_COUNT), lambda i: (0, 0, 0)),
        out_shape=jax.ShapeDtypeStruct((cap, freq_block, 2 * RAY_PARAM_COUNT), jnp.bfloat16),
        scratch_shapes=[pltpu.VMEM((2, cap * freq_block, LANES), jnp.float32)],
        compiler_params=pltpu.CompilerParams(vmem_limit_bytes=VMEM_BYTES),
        name="encode",
    )(*([held] * len(firsts)), phases, phases)


def on_device(traces, trace_counts, aperture_start, shot_position, rec_slot):
    shots = trace_counts.shape[1]
    freq_groups = lax.axis_size("freq")
    slabs = lax.axis_size("slab")
    freq_block = FREQUENCY_COUNT // freq_groups
    cap = 3 * NREC // (2 * slabs)
    axes = ("freq", "slab")
    positions = lax.all_gather(shot_position, axes, axis=0, tiled=True)
    lattice = make_lattice(
        traces, trace_counts[0], aperture_start, rec_slot, slabs, cap, freq_groups
    )
    received = lax.all_to_all(lattice, axes, split_axis=0, concat_axis=0, tiled=True)
    first_bin = (F0 + lax.axis_index("freq") * freq_block).astype(jnp.int32)[None]
    phases = make_phases(positions, first_bin, freq_block, shots)
    return encode(received, phases, cap, freq_block, shots)


def solution(mesh):
    return jax.shard_map(
        on_device,
        mesh=mesh,
        in_specs=(
            P(("freq", "slab"), None),
            P(("freq", "slab"), None),
            P(("freq", "slab")),
            P(("freq", "slab")),
            P(),
        ),
        out_specs=P("slab", "freq", None),
        check_vma=False,
    )
```

time: 697 us -> 235 us (0.34)
  waiting for transfers between devices: 416 us -> 0.01 us
  local copies, waits for them, and re-layouts: 163 us -> 1.58 us
  blocking collectives: 36.6 us -> 159 us
  Pallas kernels: 0 us -> 61.6 us
  matrix products: 44.6 us -> 0 us
  between operations: 14.2 us -> 0.04 us
  other arithmetic: 15.5 us -> 3.06 us
    reduce_scatter x1 -> x0, waiting for transfers between devices: 416 us -> none  [on_device(): lax.psum_scatter(jnp.einsum('xfs,fsq->xfq', filled_lattice, phases, prefe...]
    unnamed x1, blocking collectives: 36.6 us -> 159 us
    gather x2 -> x0, local copies, waits for them, and re-layouts: 122 us -> none  [slot_grid(): picked = jnp.take(owned_spectra, picks.reshape(-1), axis=1)]
    pallas_call x0 -> x3, Pallas kernels: none -> 61.6 us  [the longest x1 27.4 us: make_lattice(): pl.pallas_call(functools.partial(lattice_kernel, slabs, whole, rest, freq...]
    dot_general x3 -> x0, matrix products: 44.6 us -> none  [the longest x1 28.7 us: frequency_spectra(): lax.dot_general(transform, traces, (((0,), (1,)), ((), ())), preferred_el...]
    transpose x1 -> x0, local copies, waits for them, and re-layouts: 25.1 us -> none  [on_device(): jnp.einsum('xfs,fsq->xfq', filled_lattice, phases, preferred_element_type...]
    convert_element_type x2 -> x0, other arithmetic: 9.53 us -> none  [the longest x1 4.95 us: on_device(): return summed.astype(jnp.bfloat16)]
  transfers between devices with their start and end apart: 2 -> 1, of which waited for: 1 -> 0; matrix products, arithmetic and copies ran while one was open for 2% -> 0% of each run, Pallas kernels for 0% -> 7%
where the time goes in v1:
time: 235 us; the launch traced here: 233 us
  blocking collectives  159 us (68%)
  Pallas kernels  61.6 us (26%)
  starting transfers between devices  7.15 us (3%)
  other arithmetic  3.06 us (1%)
    unnamed x1, blocking collectives  159 us
    pallas_call x1, Pallas kernels, make_lattice(): pl.pallas_call(functools.partial(lattice_kernel, slabs, whole, rest, freq...  27.4 us
    pallas_call x1, Pallas kernels, encode(): pl.pallas_call(functools.partial(encode_kernel, cap, whole, rest, pair),...  17.4 us
    pallas_call x1, Pallas kernels, make_phases(): pl.pallas_call(functools.partial(phase_kernel, shots, total_shots), grid=...  16.8 us
    all_to_all x1, starting transfers between devices, on_device(): lax.all_to_all(lattice, axes, split_axis=0, concat_axis=0, tiled=True)  7.15 us
  transfers between devices with their start and end apart: 1, of which 0 were waited for; matrix products, arithmetic and copies ran while one was open for 0% of the time, Pallas kernels for 7%

profile of v1, /device:TPU:1, one launch (start us, length us, event | category | flops | bytes accessed | tf_op | source)
XLA Modules:
  0.0 232.8 jit_solution(16283426319505894415)
XLA Ops:
  0.0 0.8 reduce-window.9
  0.8 1.2 bitcast_subtract_fusion.begins
  2.1 1.0 select_reduce_fusion
  3.1 0.6 broadcast_in_dim.29.inverse
  3.6 27.4 %lattice.1 = bf16[32,768,128]{2,1,0:T(8,128)(2,1)} custom-call(s32[8]{0:T(128)} %starts.1, s32[8]{0:T(128)} %bitcast.8, s32[8]{0:T(128)} %bitcast_subtract_fusion.begins, s32[1,768]{1,0:T(1,128)} %broadcast_in_dim.29.inverse, bf16[512,2048]{1,0:T(8,128)(2,1)} %constant.23.clone.table, bf16[3072,2048]{1,0:T(8,128)(2,1)} %traces.1), custom_call_target="tpu_custom_call" | custom-call | flops 6442450944 | bytes 12582912 | tf_op jit(solution)/shard_map/lattice/pallas_call | solution.py:142
  31.0 0.0 copy-start
  31.0 7.1 %all-to-all-start = ((bf16[32,768,128]{2,1,0:T(8,128)(2,1)}), bf16[32,768,128]{2,1,0:T(8,128)(2,1)}, u32[]{:S(2)}, u32[]{:S(2)}) async-start(bf16[32,768,128]{2,1,0:T(8,128)(2,1)} %lattice.1), calls=%async_computation | async-start | bytes 12582912 | tf_op jit(solution)/shard_map/all_to_all | solution.py:324
  38.2 0.0 copy-done
  38.2 0.2 dynamic-update-slice
  38.5 159.3 %all-reduce = s32[256]{0:T(256)S(1)} all-reduce(s32[256]{0:T(256)S(1)} %dynamic-update-slice), channel_id=1, replica_groups=mesh['freq'=8,'slab'=4] {'freq','slab'}, use_global_device_ids=true, to_apply=%add | all-reduce | flops 256 | bytes 2048
  197.8 0.8 broadcast_in_dim.31.positions
  198.6 16.8 %phases.1.refs_3_.refs_4_ = bf16[32,512,256]{2,1,0:T(8,128)(2,1)} custom-call(s32[1]{0:T(128)} %bitcast.4.first_bin, s32[256,128]{1,0:T(8,128)} %broadcast_in_dim.31.positions), custom_call_target="tpu_custom_call" | custom-call | flops 41943040 | bytes 8388608 | tf_op jit(solution)/shard_map/phases/pallas_call | solution.py:215
  215.4 0.0 all-to-all-done
  215.4 17.4 %encode.1 = bf16[192,32,256]{2,1,0:T(8,128)(2,1)} custom-call(bf16[32,48,16,128]{3,2,1,0:T(8,128)(2,1)} %bitcast.3.refs_0_.refs_1_.refs_2_, bf16[32,48,16,128]{3,2,1,0:T(8,128)(2,1)} %bitcast.3.refs_0_.refs_1_.refs_2_, bf16[32,48,16,128]{3,2,1,0:T(8,128)(2,1)} %bitcast.3.refs_0_.refs_1_.refs_2_, bf16[32,512,256]{2,1,0:T(8,128)(2,1)} %phases.1.refs_3_.refs_4_, ...), custom_call_target="tpu_custom_call" | custom-call | tf_op jit(solution)/shard_map/encode/pallas_call | solution.py:297
  (1 shorter events, 0.0 us)
Async XLA Ops:
  31.0 7.2 %copy-start = (s32[8]{0:T(128)S(1)}, s32[8]{0:T(128)}, u32[]{:S(2)}) copy-start(s32[8]{0:T(128)} %param.10) | copy-start | bytes 100
  31.0 184.4 %all-to-all-start = ((bf16[32,768,128]{2,1,0:T(8,128)(2,1)}), bf16[32,768,128]{2,1,0:T(8,128)(2,1)}, u32[]{:S(2)}, u32[]{:S(2)}) async-start(bf16[32,768,128]{2,1,0:T(8,128)(2,1)} %lattice.1), calls=%async_computation | async-start | bytes 12582912 | tf_op jit(solution)/shard_map/all_to_all | solution.py:324
